TPU v7x, 256 devices: a whole 4x4x8 slice. The times are simulated.
256 devices in a mesh: view: 8 (over z), wide: 32 (over y, x, core).
Axes of the slice: x: 4, y: 4, z: 8, core: 2. Of those that a mesh axis runs over, the one named last changes fastest.
Arguments:
- tracer: float32 [512, 1024, 128], P('view', 'wide'), may hold values from 0.05 to 5
- velocity: float32 [3, 512, 1024, 128], P(None, 'view', 'wide'), may hold values from -0.15 to 0.15
- buildings: int32 [512, 1024, 128], P('view', 'wide'), may hold values from 0 to 1, as said below
- source: float32 [512, 1024, 128], P('view', 'wide'), may hold values from 0 to 0.5
Outputs:
- tracer_next: float32 [512, 1024, 128], P('view', 'wide')
- picture: float32 [4, 1024, 128], P(None, 'wide', 'view')
Inputs may be any that keep to these rules, and one draw needn't show every extreme that they name: `buildings`: each column of cells at a fixed first and second index is inside a building from the ground up to some height of at most 64 cells, and outside above it.
All inputs are finite; a program needn't handle non-finite values.
Results may differ from a plain program's by a relative error of at most 0.000056.
Values sent between devices are 32-bit elements; how exact they have to be, the bound alone decides.
A program may use at most 64 MiB of HBM per device.

v0:
```python
import jax
import jax.numpy as jnp
from jax import lax
from jax.sharding import PartitionSpec as P

STEPS = 4


def padded_2(cells, sides, width):
    for axis, dim in sides:
        count = lax.axis_size(axis)
        head = lax.slice_in_dim(cells, 0, width, axis=dim)
        tail = lax.slice_in_dim(cells, cells.shape[dim] - width, cells.shape[dim], axis=dim)
        cells = jnp.concatenate(
            [
                lax.ppermute(tail, axis, [(i, (i + 1) % count) for i in range(count)]),
                cells,
                lax.ppermute(head, axis, [((i + 1) % count, i) for i in range(count)]),
            ],
            axis=dim,
        )
    return cells


def advance(tracer, velocity, open_cells, source):
    face_zero = velocity[0][:-1] * open_cells[:-1] * open_cells[1:]
    flux_zero = jnp.maximum(face_zero, 0.0) * tracer[:-1] + jnp.minimum(face_zero, 0.0) * tracer[1:]
    delta_zero = (flux_zero[1:] - flux_zero[:-1])[:, 1:-1]
    face_one = velocity[1][:, :-1] * open_cells[:, :-1] * open_cells[:, 1:]
    flux_one = (
        jnp.maximum(face_one, 0.0) * tracer[:, :-1] + jnp.minimum(face_one, 0.0) * tracer[:, 1:]
    )
    delta_one = (flux_one[:, 1:] - flux_one[:, :-1])[1:-1]
    face_two = velocity[2][:, :, :-1] * open_cells[:, :, :-1] * open_cells[:, :, 1:]
    flux_two = (
        jnp.maximum(face_two, 0.0) * tracer[:, :, :-1]
        + jnp.minimum(face_two, 0.0) * tracer[:, :, 1:]
    )
    padded = jnp.pad(flux_two, ((0, 0), (0, 0), (1, 1)))
    delta_two = (padded[:, :, 1:] - padded[:, :, :-1])[1:-1, 1:-1]
    inner_tracer = tracer[1:-1, 1:-1]
    return open_cells[1:-1, 1:-1] * (
        inner_tracer - delta_zero - delta_one - delta_two + source[1:-1, 1:-1]
    )


def shade_cells(tracer, open_cells):
    shading = tracer / (1.0 + tracer)
    walls = 1.0 - open_cells
    red = open_cells * shading + 0.55 * walls
    green = open_cells * jnp.exp(-0.5 * tracer) + 0.5 * walls
    blue = open_cells * (0.2 + 0.6 * shading * shading) + 0.45 * walls
    return (red, green, blue)


def composite(nearer, farther):
    colors = nearer[:3] + nearer[3:] * farther[:3]
    return jnp.concatenate([colors, nearer[3:] * farther[3:]], axis=0)


def fold_in_order(layers):
    start_value = jnp.concatenate(
        [
            jnp.zeros((3,) + layers.shape[2:], jnp.float32),
            jnp.ones((1,) + layers.shape[2:], jnp.float32),
        ],
        axis=0,
    )

    def fold_step(running, layer_piece):
        return (composite(running, layer_piece), None)

    result, unused = lax.scan(fold_step, start_value, layers)
    return result


def finish_pixels(result):
    return jnp.concatenate([result[:3], 1.0 - result[3:]], axis=0)


def march_steps(tracer, speeds, open_wide, source_wide):
    current = tracer
    for substep in range(STEPS):
        tracer_wide = padded_2(current, (("view", 0), ("wide", 1)), 1)
        current = advance(tracer_wide, speeds, open_wide, source_wide)
    return current


def on_device(tracer, velocity, buildings, source):
    open_cells = (1 - buildings).astype(jnp.float32)
    static = jnp.concatenate([velocity, open_cells[None], source[None]], axis=0)
    grown_static = padded_2(static, (("view", 1), ("wide", 2)), 1)
    current = march_steps(tracer, grown_static[:3], grown_static[3], grown_static[4])
    view_count = lax.axis_size("view")
    depth_cells = float(tracer.shape[0] * view_count)
    extinction = (current * open_cells + 4.0 * (1.0 - open_cells)) / depth_cells
    before = jnp.cumsum(extinction, axis=0) - extinction
    weight = jnp.exp(-before) * (1.0 - jnp.exp(-extinction))
    red, green, blue = shade_cells(current, open_cells)
    partial_value = jnp.stack(
        [
            jnp.sum(weight * red, axis=0),
            jnp.sum(weight * green, axis=0),
            jnp.sum(weight * blue, axis=0),
            jnp.exp(-jnp.sum(extinction, axis=0)),
        ]
    )
    height = partial_value.shape[2]
    block_width = height // view_count
    position = lax.axis_index("view")
    pieces = lax.all_gather(partial_value[None], "view", axis=0, tiled=True)
    mine = lax.dynamic_slice_in_dim(pieces, position * block_width, block_width, 3)
    picture = finish_pixels(fold_in_order(mine))
    return (current, picture)


def solution(mesh):
    return jax.shard_map(
        on_device,
        mesh=mesh,
        in_specs=(
            P("view", "wide", None),
            P(None, "view", "wide", None),
            P("view", "wide", None),
            P("view", "wide", None),
        ),
        out_specs=(P("view", "wide", None), P(None, "wide", "view")),
        check_vma=False,
    )
```

profile of v0, /device:TPU:32, one launch (start us, length us, event | category | flops | bytes accessed | tf_op | source)
XLA Modules:
  0.0 111.1 jit_solution(14347198532158714569)
XLA Ops:
  1.5 1.8 %collective-permute-start.5 = (f32[1,32,128]{2,1,0:T(8,128)S(1)}, f32[1,32,128]{2,1,0:T(8,128)S(1)}, u32[]{:S(2)}, u32[]{:S(2)}) collective-permute-start(f32[1,32,128]{2,1,0:T(8,128)S(1)} %get-tuple-element.84), channel_id=1, source_target_pairs={{32,0},{64,32},{96,64},{128,96},{160,128},{192,160},{224,192},{0,2... | collective-permute-start | bytes 49160 | tf_op jit(solution)/shard_map/ppermute | solution.py:18
  3.5 1.3 %convert_bitcast_fusion = f32[1,64,32,128]{3,2,1,0:T(8,128)S(1)} fusion(s32[64,32,128]{2,1,0:T(8,128)} %param.8), kind=kLoop, calls=%fused_computation.110 | loop fusion | flops 524288 | bytes 2097152 | tf_op jit(solution)/shard_map/broadcast_in_dim | solution.py:91
  4.9 1.0 pad_maximum_fusion.13
  5.9 2.0 %collective-permute-start = (f32[5,1,32,128]{3,2,1,0:T(8,128)S(1)}, f32[5,1,32,128]{3,2,1,0:T(8,128)S(1)}, u32[]{:S(2)}, u32[]{:S(2)}) collective-permute-start(f32[5,1,32,128]{3,2,1,0:T(8,128)S(1)} %get-tuple-element.44), channel_id=1, source_target_pairs={{0,32},{32,64},{64,96},{96,128},{128,160},{160,192},{192,224},{224... | collective-permute-start | bytes 245768 | tf_op jit(solution)/shard_map/ppermute | solution.py:16
  7.9 2.1 %collective-permute-start.1 = (f32[5,1,32,128]{3,2,1,0:T(8,128)S(1)}, f32[5,1,32,128]{3,2,1,0:T(8,128)S(1)}, u32[]{:S(2)}, u32[]{:S(2)}) collective-permute-start(f32[5,1,32,128]{3,2,1,0:T(8,128)S(1)} %get-tuple-element.45), channel_id=1, source_target_pairs={{32,0},{64,32},{96,64},{128,96},{160,128},{192,160},{224,192},{0,2... | collective-permute-start | bytes 245768 | tf_op jit(solution)/shard_map/ppermute | solution.py:18
  10.2 5.1 %collective-permute-start.7 = (f32[66,1,128]{2,1,0:T(1,128)S(1)}, f32[66,1,128]{2,1,0:T(1,128)S(1)}, u32[]{:S(2)}, u32[]{:S(2)}) collective-permute-start(f32[66,1,128]{2,1,0:T(1,128)S(1)} %get-tuple-element.77), channel_id=1, source_target_pairs={{1,0},{2,1},{3,2},{4,3},{5,4},{6,5},{7,6},{8,7},{9,8},{10,9},{11,1... | collective-permute-start | bytes 101384 | tf_op jit(solution)/shard_map/ppermute | solution.py:18
  15.6 5.1 %collective-permute-start.3 = (f32[5,66,1,128]{3,2,1,0:T(1,128)S(1)}, f32[5,66,1,128]{3,2,1,0:T(1,128)S(1)}, u32[]{:S(2)}, u32[]{:S(2)}) collective-permute-start(f32[5,66,1,128]{3,2,1,0:T(1,128)S(1)} %get-tuple-element.43), channel_id=1, source_target_pairs={{1,0},{2,1},{3,2},{4,3},{5,4},{6,5},{7,6},{8,7},{9,8},{10,9},{11,1... | collective-permute-start | bytes 506888 | tf_op jit(solution)/shard_map/ppermute | solution.py:18
  20.9 2.8 %collective-permute-done.2 = f32[5,66,1,128]{3,2,1,0:T(1,128)S(1)} collective-permute-done((f32[5,66,1,128]{3,2,1,0:T(1,128)S(1)}, f32[5,66,1,128]{3,2,1,0:T(1,128)S(1)}, u32[]{:S(2)}, u32[]{:S(2)}) %collective-permute-start.2) | collective-permute-done | bytes 168992 | tf_op jit(solution)/shard_map/ppermute | solution.py:16
  23.7 2.7 %pad_maximum_fusion.1 = f32[5,66,34,128]{3,2,1,0:T(8,128)S(1)} fusion(f32[5,66,1,128]{3,2,1,0:T(1,128)S(1)} %collective-permute-done.3, f32[5,1,32,128]{3,2,1,0:T(8,128)S(1)} %collective-permute-done.1, f32[1,64,32,128]{3,2,1,0:T(8,128)S(1)} %bitcast.45, f32[1,64,32,128]{3,2,1,0:T(8,128)S(1)} %convert_bitcast_fusion, f32[3,64,32,128]{3,2,1,0:T(8,128)S(1)} %copy-done, ...), kind=kLoop, calls=%fused_computation.7 | loop fusion | flops 8616960 | bytes 11489280 | tf_op jit(solution)/shard_map/concatenate | solution.py:14
  29.5 0.9 fusion.37
  30.4 1.3 %collective-permute-start.8 = (f32[1,32,128]{2,1,0:T(8,128)S(1)}, f32[1,32,128]{2,1,0:T(8,128)S(1)}, u32[]{:S(2)}, u32[]{:S(2)}) collective-permute-start(f32[1,32,128]{2,1,0:T(8,128)S(1)} %get-tuple-element.82), channel_id=1, source_target_pairs={{0,32},{32,64},{64,96},{96,128},{128,160},{160,192},{192,224},{224... | collective-permute-start | bytes 49160 | tf_op jit(solution)/shard_map/ppermute | solution.py:16
  31.7 2.3 %collective-permute-start.9 = (f32[1,32,128]{2,1,0:T(8,128)S(1)}, f32[1,32,128]{2,1,0:T(8,128)S(1)}, u32[]{:S(2)}, u32[]{:S(2)}) collective-permute-start(f32[1,32,128]{2,1,0:T(8,128)S(1)} %get-tuple-element.83), channel_id=1, source_target_pairs={{32,0},{64,32},{96,64},{128,96},{160,128},{192,160},{224,192},{0,2... | collective-permute-start | bytes 49160 | tf_op jit(solution)/shard_map/ppermute | solution.py:18
  34.0 1.6 %collective-permute-done.8 = f32[1,32,128]{2,1,0:T(8,128)S(1)} collective-permute-done((f32[1,32,128]{2,1,0:T(8,128)S(1)}, f32[1,32,128]{2,1,0:T(8,128)S(1)}, u32[]{:S(2)}, u32[]{:S(2)}) %collective-permute-start.8) | collective-permute-done | bytes 16416 | tf_op jit(solution)/shard_map/ppermute | solution.py:16
  35.7 5.1 %collective-permute-start.11 = (f32[66,1,128]{2,1,0:T(1,128)S(1)}, f32[66,1,128]{2,1,0:T(1,128)S(1)}, u32[]{:S(2)}, u32[]{:S(2)}) collective-permute-start(f32[66,1,128]{2,1,0:T(1,128)S(1)} %get-tuple-element.75), channel_id=1, source_target_pairs={{1,0},{2,1},{3,2},{4,3},{5,4},{6,5},{7,6},{8,7},{9,8},{10,9},{11,1... | collective-permute-start | bytes 101384 | tf_op jit(solution)/shard_map/ppermute | solution.py:18
  40.8 1.6 %collective-permute-done.10 = f32[66,1,128]{2,1,0:T(1,128)S(1)} collective-permute-done((f32[66,1,128]{2,1,0:T(1,128)S(1)}, f32[66,1,128]{2,1,0:T(1,128)S(1)}, u32[]{:S(2)}, u32[]{:S(2)}) %collective-permute-start.10) | collective-permute-done | bytes 33824 | tf_op jit(solution)/shard_map/ppermute | solution.py:16
  44.6 1.1 %fusion.32 = f32[64,32,128]{2,1,0:T(8,128)S(1)} fusion(f32[66,34,128]{2,1,0:T(8,128)S(1)} %get-tuple-element.57, f32[66,34,128]{2,1,0:T(8,128)S(1)} %get-tuple-element.56, f32[66,32,128]{2,1,0:T(8,128)S(1)} %get-tuple-element.55, f32[66,32,128]{2,1,0:T(8,128)S(1)} %get-tuple-element.54, f32[64,32,128]{2,1,0:T(8,128)S(1)} %fusion.37, ...), kind=kLoop, calls=%fused_computation.92 | loop fusion | flops 2097152 | bytes 10485760 | tf_op jit(solution)/shard_map/mul | solution.py:42
  45.7 3.0 %collective-permute-start.12 = (f32[1,32,128]{2,1,0:T(8,128)S(1)}, f32[1,32,128]{2,1,0:T(8,128)S(1)}, u32[]{:S(2)}, u32[]{:S(2)}) collective-permute-start(f32[1,32,128]{2,1,0:T(8,128)S(1)} %get-tuple-element.80), channel_id=1, source_target_pairs={{0,32},{32,64},{64,96},{96,128},{128,160},{160,192},{192,224},{224... | collective-permute-start | bytes 49160 | tf_op jit(solution)/shard_map/ppermute | solution.py:16
  49.1 1.6 %collective-permute-done.12 = f32[1,32,128]{2,1,0:T(8,128)S(1)} collective-permute-done((f32[1,32,128]{2,1,0:T(8,128)S(1)}, f32[1,32,128]{2,1,0:T(8,128)S(1)}, u32[]{:S(2)}, u32[]{:S(2)}) %collective-permute-start.12) | collective-permute-done | bytes 16416 | tf_op jit(solution)/shard_map/ppermute | solution.py:16
  50.7 2.9 %collective-permute-done.13 = f32[1,32,128]{2,1,0:T(8,128)S(1)} collective-permute-done((f32[1,32,128]{2,1,0:T(8,128)S(1)}, f32[1,32,128]{2,1,0:T(8,128)S(1)}, u32[]{:S(2)}, u32[]{:S(2)}) %collective-permute-start.13) | collective-permute-done | bytes 16416 | tf_op jit(solution)/shard_map/ppermute | solution.py:18
  53.8 5.1 %collective-permute-start.15 = (f32[66,1,128]{2,1,0:T(1,128)S(1)}, f32[66,1,128]{2,1,0:T(1,128)S(1)}, u32[]{:S(2)}, u32[]{:S(2)}) collective-permute-start(f32[66,1,128]{2,1,0:T(1,128)S(1)} %get-tuple-element.73), channel_id=1, source_target_pairs={{1,0},{2,1},{3,2},{4,3},{5,4},{6,5},{7,6},{8,7},{9,8},{10,9},{11,1... | collective-permute-start | bytes 101384 | tf_op jit(solution)/shard_map/ppermute | solution.py:18
  58.8 1.6 %collective-permute-done.14 = f32[66,1,128]{2,1,0:T(1,128)S(1)} collective-permute-done((f32[66,1,128]{2,1,0:T(1,128)S(1)}, f32[66,1,128]{2,1,0:T(1,128)S(1)}, u32[]{:S(2)}, u32[]{:S(2)}) %collective-permute-start.14) | collective-permute-done | bytes 33824 | tf_op jit(solution)/shard_map/ppermute | solution.py:16
  62.7 1.2 %fusion.27 = f32[64,32,128]{2,1,0:T(8,128)S(1)} fusion(f32[66,34,128]{2,1,0:T(8,128)S(1)} %get-tuple-element.53, f32[66,34,128]{2,1,0:T(8,128)S(1)} %get-tuple-element.52, f32[66,32,128]{2,1,0:T(8,128)S(1)} %get-tuple-element.51, f32[66,32,128]{2,1,0:T(8,128)S(1)} %get-tuple-element.50, f32[64,32,128]{2,1,0:T(8,128)S(1)} %fusion.32, ...), kind=kLoop, calls=%fused_computation.84 | loop fusion | flops 2097152 | bytes 10485760 | tf_op jit(solution)/shard_map/mul | solution.py:42
  63.9 2.1 %collective-permute-start.16 = (f32[1,32,128]{2,1,0:T(8,128)S(1)}, f32[1,32,128]{2,1,0:T(8,128)S(1)}, u32[]{:S(2)}, u32[]{:S(2)}) collective-permute-start(f32[1,32,128]{2,1,0:T(8,128)S(1)} %get-tuple-element.78), channel_id=1, source_target_pairs={{0,32},{32,64},{64,96},{96,128},{128,160},{160,192},{192,224},{224... | collective-permute-start | bytes 49160 | tf_op jit(solution)/shard_map/ppermute | solution.py:16
  66.0 1.7 %collective-permute-done.16 = f32[1,32,128]{2,1,0:T(8,128)S(1)} collective-permute-done((f32[1,32,128]{2,1,0:T(8,128)S(1)}, f32[1,32,128]{2,1,0:T(8,128)S(1)}, u32[]{:S(2)}, u32[]{:S(2)}) %collective-permute-start.16) | collective-permute-done | bytes 16416 | tf_op jit(solution)/shard_map/ppermute | solution.py:16
  67.7 2.0 %collective-permute-done.17 = f32[1,32,128]{2,1,0:T(8,128)S(1)} collective-permute-done((f32[1,32,128]{2,1,0:T(8,128)S(1)}, f32[1,32,128]{2,1,0:T(8,128)S(1)}, u32[]{:S(2)}, u32[]{:S(2)}) %collective-permute-start.17) | collective-permute-done | bytes 16416 | tf_op jit(solution)/shard_map/ppermute | solution.py:18
  69.8 5.1 %collective-permute-start.19 = (f32[66,1,128]{2,1,0:T(1,128)S(1)}, f32[66,1,128]{2,1,0:T(1,128)S(1)}, u32[]{:S(2)}, u32[]{:S(2)}) collective-permute-start(f32[66,1,128]{2,1,0:T(1,128)S(1)} %get-tuple-element.71), channel_id=1, source_target_pairs={{1,0},{2,1},{3,2},{4,3},{5,4},{6,5},{7,6},{8,7},{9,8},{10,9},{11,1... | collective-permute-start | bytes 101384 | tf_op jit(solution)/shard_map/ppermute | solution.py:18
  74.9 1.6 %collective-permute-done.18 = f32[66,1,128]{2,1,0:T(1,128)S(1)} collective-permute-done((f32[66,1,128]{2,1,0:T(1,128)S(1)}, f32[66,1,128]{2,1,0:T(1,128)S(1)}, u32[]{:S(2)}, u32[]{:S(2)}) %collective-permute-start.18) | collective-permute-done | bytes 33824 | tf_op jit(solution)/shard_map/ppermute | solution.py:16
  77.0 1.0 copy-done.6
  78.5 0.9 copy-done.4
  81.5 1.0 fusion.22
  82.7 1.4 %multiply_reduce_fusion.1 = (f32[32,128]{1,0:T(8,128)S(1)}, f32[32,128]{1,0:T(8,128)S(1)}, f32[32,128]{1,0:T(8,128)S(1)}, f32[32,128]{1,0:T(8,128)S(1)}) fusion(s32[64,32,128]{2,1,0:T(8,128)S(1)} %copy-done.10, f32[64,32,128]{2,1,0:T(8,128)S(1)} %fusion.22), kind=kOutput, calls=%fused_computation.106 | output fusion | flops 27246592 | bytes 2162688 | tf_op jit(solution)/shard_map/jit(cumsum)/reduce_window_sum | solution.py:97
  84.1 25.4 %all-gather = f32[32,32,128]{2,1,0:T(8,128)S(1)} all-gather(f32[4,32,128]{2,1,0:T(8,128)S(1)} %pad_maximum_fusion.14), channel_id=2, replica_groups=mesh['view'=8,'wide'=32] {'view'}, dimensions={0}, use_global_device_ids=true | all-gather | bytes 589824 | tf_op jit(solution)/shard_map/all_gather | solution.py:111
  (118 shorter events, 14.9 us)
Async XLA Ops:
  0.6 4.2 %copy-start.11 = (f32[64,32,128]{2,1,0:T(8,128)S(1)}, f32[64,32,128]{2,1,0:T(8,128)}, u32[]{:S(2)}) copy-start(f32[64,32,128]{2,1,0:T(8,128)} %param.9) | copy-start | bytes 3145732
  1.5 8.6 %collective-permute-start.5 = (f32[1,32,128]{2,1,0:T(8,128)S(1)}, f32[1,32,128]{2,1,0:T(8,128)S(1)}, u32[]{:S(2)}, u32[]{:S(2)}) collective-permute-start(f32[1,32,128]{2,1,0:T(8,128)S(1)} %get-tuple-element.84), channel_id=1, source_target_pairs={{32,0},{64,32},{96,64},{128,96},{160,128},{192,160},{224,192},{0,2... | collective-permute-start | bytes 49160 | tf_op jit(solution)/shard_map/ppermute | solution.py:18
  3.3 6.7 %collective-permute-start.4 = (f32[1,32,128]{2,1,0:T(8,128)S(1)}, f32[1,32,128]{2,1,0:T(8,128)S(1)}, u32[]{:S(2)}, u32[]{:S(2)}) collective-permute-start(f32[1,32,128]{2,1,0:T(8,128)S(1)} %get-tuple-element.85), channel_id=1, source_target_pairs={{0,32},{32,64},{64,96},{96,128},{128,160},{160,192},{192,224},{224... | collective-permute-start | bytes 49160 | tf_op jit(solution)/shard_map/ppermute | solution.py:16
  4.8 5.1 %copy-start.12 = (f32[64,32,128]{2,1,0:T(8,128)S(1)}, f32[64,32,128]{2,1,0:T(8,128)}, u32[]{:S(2)}) copy-start(f32[64,32,128]{2,1,0:T(8,128)} %param.6) | copy-start | bytes 3145732
  4.9 10.4 %copy-start = (f32[3,64,32,128]{3,2,1,0:T(8,128)S(1)}, f32[3,64,32,128]{3,2,1,0:T(8,128)}, u32[]{:S(2)}) copy-start(f32[3,64,32,128]{3,2,1,0:T(8,128)} %param.7) | copy-start | bytes 9437188
  5.9 9.4 %collective-permute-start = (f32[5,1,32,128]{3,2,1,0:T(8,128)S(1)}, f32[5,1,32,128]{3,2,1,0:T(8,128)S(1)}, u32[]{:S(2)}, u32[]{:S(2)}) collective-permute-start(f32[5,1,32,128]{3,2,1,0:T(8,128)S(1)} %get-tuple-element.44), channel_id=1, source_target_pairs={{0,32},{32,64},{64,96},{96,128},{128,160},{160,192},{192,224},{224... | collective-permute-start | bytes 245768 | tf_op jit(solution)/shard_map/ppermute | solution.py:16
  7.9 7.4 %collective-permute-start.1 = (f32[5,1,32,128]{3,2,1,0:T(8,128)S(1)}, f32[5,1,32,128]{3,2,1,0:T(8,128)S(1)}, u32[]{:S(2)}, u32[]{:S(2)}) collective-permute-start(f32[5,1,32,128]{3,2,1,0:T(8,128)S(1)} %get-tuple-element.45), channel_id=1, source_target_pairs={{32,0},{64,32},{96,64},{128,96},{160,128},{192,160},{224,192},{0,2... | collective-permute-start | bytes 245768 | tf_op jit(solution)/shard_map/ppermute | solution.py:18
  10.1 10.5 %collective-permute-start.6 = (f32[66,1,128]{2,1,0:T(1,128)S(1)}, f32[66,1,128]{2,1,0:T(1,128)S(1)}, u32[]{:S(2)}, u32[]{:S(2)}) collective-permute-start(f32[66,1,128]{2,1,0:T(1,128)S(1)} %get-tuple-element.76), channel_id=1, source_target_pairs={{0,1},{1,2},{2,3},{3,4},{4,5},{5,6},{6,7},{7,8},{8,9},{9,10},{10,1... | collective-permute-start | bytes 101384 | tf_op jit(solution)/shard_map/ppermute | solution.py:16
  10.2 10.5 %collective-permute-start.7 = (f32[66,1,128]{2,1,0:T(1,128)S(1)}, f32[66,1,128]{2,1,0:T(1,128)S(1)}, u32[]{:S(2)}, u32[]{:S(2)}) collective-permute-start(f32[66,1,128]{2,1,0:T(1,128)S(1)} %get-tuple-element.77), channel_id=1, source_target_pairs={{1,0},{2,1},{3,2},{4,3},{5,4},{6,5},{7,6},{8,7},{9,8},{10,9},{11,1... | collective-permute-start | bytes 101384 | tf_op jit(solution)/shard_map/ppermute | solution.py:18
  15.5 8.2 %collective-permute-start.2 = (f32[5,66,1,128]{3,2,1,0:T(1,128)S(1)}, f32[5,66,1,128]{3,2,1,0:T(1,128)S(1)}, u32[]{:S(2)}, u32[]{:S(2)}) collective-permute-start(f32[5,66,1,128]{3,2,1,0:T(1,128)S(1)} %get-tuple-element.42), channel_id=1, source_target_pairs={{0,1},{1,2},{2,3},{3,4},{4,5},{5,6},{6,7},{7,8},{8,9},{9,10},{10,1... | collective-permute-start | bytes 506888 | tf_op jit(solution)/shard_map/ppermute | solution.py:16
  15.6 8.1 %collective-permute-start.3 = (f32[5,66,1,128]{3,2,1,0:T(1,128)S(1)}, f32[5,66,1,128]{3,2,1,0:T(1,128)S(1)}, u32[]{:S(2)}, u32[]{:S(2)}) collective-permute-start(f32[5,66,1,128]{3,2,1,0:T(1,128)S(1)} %get-tuple-element.43), channel_id=1, source_target_pairs={{1,0},{2,1},{3,2},{4,3},{5,4},{6,5},{7,6},{8,7},{9,8},{10,9},{11,1... | collective-permute-start | bytes 506888 | tf_op jit(solution)/shard_map/ppermute | solution.py:18
  26.9 35.8 %copy-start.1 = (f32[66,34,128]{2,1,0:T(8,128)}, f32[66,34,128]{2,1,0:T(8,128)S(1)}, u32[]{:S(2)}) copy-start(f32[66,34,128]{2,1,0:T(8,128)S(1)} %get-tuple-element.38) | copy-start | bytes 3446788
  27.2 33.5 %copy-start.7 = (f32[1,65,34,128]{3,2,1,0:T(8,128)}, f32[1,65,34,128]{3,2,1,0:T(8,128)S(1)}, u32[]{:S(2)}) copy-start(f32[1,65,34,128]{3,2,1,0:T(8,128)S(1)} %get-tuple-element.31) | copy-start | bytes 3394564
  27.7 33.7 %copy-start.3 = (f32[66,33,128]{2,1,0:T(8,128)}, f32[66,33,128]{2,1,0:T(8,128)S(1)}, u32[]{:S(2)}) copy-start(f32[66,33,128]{2,1,0:T(8,128)S(1)} %get-tuple-element.33) | copy-start | bytes 3345412
  29.0 31.9 %copy-start.5 = (f32[66,34,127]{2,1,0:T(8,128)}, f32[66,34,127]{2,1,0:T(8,128)S(1)}, u32[]{:S(2)}) copy-start(f32[66,34,127]{2,1,0:T(8,128)S(1)} %get-tuple-element.35) | copy-start | bytes 3419860
  30.4 5.2 %collective-permute-start.8 = (f32[1,32,128]{2,1,0:T(8,128)S(1)}, f32[1,32,128]{2,1,0:T(8,128)S(1)}, u32[]{:S(2)}, u32[]{:S(2)}) collective-permute-start(f32[1,32,128]{2,1,0:T(8,128)S(1)} %get-tuple-element.82), channel_id=1, source_target_pairs={{0,32},{32,64},{64,96},{96,128},{128,160},{160,192},{192,224},{224... | collective-permute-start | bytes 49160 | tf_op jit(solution)/shard_map/ppermute | solution.py:16
  31.7 3.9 %collective-permute-start.9 = (f32[1,32,128]{2,1,0:T(8,128)S(1)}, f32[1,32,128]{2,1,0:T(8,128)S(1)}, u32[]{:S(2)}, u32[]{:S(2)}) collective-permute-start(f32[1,32,128]{2,1,0:T(8,128)S(1)} %get-tuple-element.83), channel_id=1, source_target_pairs={{32,0},{64,32},{96,64},{128,96},{160,128},{192,160},{224,192},{0,2... | collective-permute-start | bytes 49160 | tf_op jit(solution)/shard_map/ppermute | solution.py:18
  35.7 6.7 %collective-permute-start.10 = (f32[66,1,128]{2,1,0:T(1,128)S(1)}, f32[66,1,128]{2,1,0:T(1,128)S(1)}, u32[]{:S(2)}, u32[]{:S(2)}) collective-permute-start(f32[66,1,128]{2,1,0:T(1,128)S(1)} %get-tuple-element.74), channel_id=1, source_target_pairs={{0,1},{1,2},{2,3},{3,4},{4,5},{5,6},{6,7},{7,8},{8,9},{9,10},{10,1... | collective-permute-start | bytes 101384 | tf_op jit(solution)/shard_map/ppermute | solution.py:16
  35.7 6.7 %collective-permute-start.11 = (f32[66,1,128]{2,1,0:T(1,128)S(1)}, f32[66,1,128]{2,1,0:T(1,128)S(1)}, u32[]{:S(2)}, u32[]{:S(2)}) collective-permute-start(f32[66,1,128]{2,1,0:T(1,128)S(1)} %get-tuple-element.75), channel_id=1, source_target_pairs={{1,0},{2,1},{3,2},{4,3},{5,4},{6,5},{7,6},{8,7},{9,8},{10,9},{11,1... | collective-permute-start | bytes 101384 | tf_op jit(solution)/shard_map/ppermute | solution.py:18
  45.7 5.0 %collective-permute-start.12 = (f32[1,32,128]{2,1,0:T(8,128)S(1)}, f32[1,32,128]{2,1,0:T(8,128)S(1)}, u32[]{:S(2)}, u32[]{:S(2)}) collective-permute-start(f32[1,32,128]{2,1,0:T(8,128)S(1)} %get-tuple-element.80), channel_id=1, source_target_pairs={{0,32},{32,64},{64,96},{96,128},{128,160},{160,192},{192,224},{224... | collective-permute-start | bytes 49160 | tf_op jit(solution)/shard_map/ppermute | solution.py:16
  48.7 4.9 %collective-permute-start.13 = (f32[1,32,128]{2,1,0:T(8,128)S(1)}, f32[1,32,128]{2,1,0:T(8,128)S(1)}, u32[]{:S(2)}, u32[]{:S(2)}) collective-permute-start(f32[1,32,128]{2,1,0:T(8,128)S(1)} %get-tuple-element.81), channel_id=1, source_target_pairs={{32,0},{64,32},{96,64},{128,96},{160,128},{192,160},{224,192},{0,2... | collective-permute-start | bytes 49160 | tf_op jit(solution)/shard_map/ppermute | solution.py:18
  53.7 6.7 %collective-permute-start.14 = (f32[66,1,128]{2,1,0:T(1,128)S(1)}, f32[66,1,128]{2,1,0:T(1,128)S(1)}, u32[]{:S(2)}, u32[]{:S(2)}) collective-permute-start(f32[66,1,128]{2,1,0:T(1,128)S(1)} %get-tuple-element.72), channel_id=1, source_target_pairs={{0,1},{1,2},{2,3},{3,4},{4,5},{5,6},{6,7},{7,8},{8,9},{9,10},{10,1... | collective-permute-start | bytes 101384 | tf_op jit(solution)/shard_map/ppermute | solution.py:16
  53.8 6.7 %collective-permute-start.15 = (f32[66,1,128]{2,1,0:T(1,128)S(1)}, f32[66,1,128]{2,1,0:T(1,128)S(1)}, u32[]{:S(2)}, u32[]{:S(2)}) collective-permute-start(f32[66,1,128]{2,1,0:T(1,128)S(1)} %get-tuple-element.73), channel_id=1, source_target_pairs={{1,0},{2,1},{3,2},{4,3},{5,4},{6,5},{7,6},{8,7},{9,8},{10,9},{11,1... | collective-permute-start | bytes 101384 | tf_op jit(solution)/shard_map/ppermute | solution.py:18
  63.9 3.8 %collective-permute-start.16 = (f32[1,32,128]{2,1,0:T(8,128)S(1)}, f32[1,32,128]{2,1,0:T(8,128)S(1)}, u32[]{:S(2)}, u32[]{:S(2)}) collective-permute-start(f32[1,32,128]{2,1,0:T(8,128)S(1)} %get-tuple-element.78), channel_id=1, source_target_pairs={{0,32},{32,64},{64,96},{96,128},{128,160},{160,192},{192,224},{224... | collective-permute-start | bytes 49160 | tf_op jit(solution)/shard_map/ppermute | solution.py:16
  66.0 3.7 %collective-permute-start.17 = (f32[1,32,128]{2,1,0:T(8,128)S(1)}, f32[1,32,128]{2,1,0:T(8,128)S(1)}, u32[]{:S(2)}, u32[]{:S(2)}) collective-permute-start(f32[1,32,128]{2,1,0:T(8,128)S(1)} %get-tuple-element.79), channel_id=1, source_target_pairs={{32,0},{64,32},{96,64},{128,96},{160,128},{192,160},{224,192},{0,2... | collective-permute-start | bytes 49160 | tf_op jit(solution)/shard_map/ppermute | solution.py:18
  69.7 6.7 %collective-permute-start.18 = (f32[66,1,128]{2,1,0:T(1,128)S(1)}, f32[66,1,128]{2,1,0:T(1,128)S(1)}, u32[]{:S(2)}, u32[]{:S(2)}) collective-permute-start(f32[66,1,128]{2,1,0:T(1,128)S(1)} %get-tuple-element.70), channel_id=1, source_target_pairs={{0,1},{1,2},{2,3},{3,4},{4,5},{5,6},{6,7},{7,8},{8,9},{9,10},{10,1... | collective-permute-start | bytes 101384 | tf_op jit(solution)/shard_map/ppermute | solution.py:16
  69.8 6.7 %collective-permute-start.19 = (f32[66,1,128]{2,1,0:T(1,128)S(1)}, f32[66,1,128]{2,1,0:T(1,128)S(1)}, u32[]{:S(2)}, u32[]{:S(2)}) collective-permute-start(f32[66,1,128]{2,1,0:T(1,128)S(1)} %get-tuple-element.71), channel_id=1, source_target_pairs={{1,0},{2,1},{3,2},{4,3},{5,4},{6,5},{7,6},{8,7},{9,8},{10,9},{11,1... | collective-permute-start | bytes 101384 | tf_op jit(solution)/shard_map/ppermute | solution.py:18
  74.9 1.8 %copy-start.8 = (f32[1,65,34,128]{3,2,1,0:T(8,128)S(1)}, f32[1,65,34,128]{3,2,1,0:T(8,128)}, u32[]{:S(2)}) copy-start(f32[1,65,34,128]{3,2,1,0:T(8,128)} %copy-done.7) | copy-start | bytes 3394564
  76.7 1.3 %copy-start.6 = (f32[66,34,127]{2,1,0:T(8,128)S(1)}, f32[66,34,127]{2,1,0:T(8,128)}, u32[]{:S(2)}) copy-start(f32[66,34,127]{2,1,0:T(8,128)} %copy-done.5) | copy-start | bytes 3419860
  80.2 1.3 %copy-start.2 = (f32[66,34,128]{2,1,0:T(8,128)S(1)}, f32[66,34,128]{2,1,0:T(8,128)}, u32[]{:S(2)}) copy-start(f32[66,34,128]{2,1,0:T(8,128)} %copy-done.1) | copy-start | bytes 3446788
  82.7 1.4 %copy-start.9 = (f32[64,32,128]{2,1,0:T(8,128)}, f32[64,32,128]{2,1,0:T(8,128)S(1)}, u32[]{:S(2)}) copy-start(f32[64,32,128]{2,1,0:T(8,128)S(1)} %fusion.22) | copy-start | bytes 3145732
  84.1 25.8 %copy-start.13 = (f32[4,32,16]{1,2,0:T(8,128)S(1)}, f32[4,32,16]{1,2,0:T(8,128)}, u32[]{:S(2)}) copy-start(f32[4,32,16]{1,2,0:T(8,128)} %constant.9.clone.1) | copy-start | bytes 24580
  (2 other events, 2.6 us)
where the time goes:
time: 111 us
  starting transfers between devices  40.9 us (37%)
  blocking collectives  25.4 us (23%)
  other arithmetic  17.7 us (16%)
  waiting for transfers between devices  17.6 us (16%)
  local copies, waits for them, and re-layouts  8.11 us (7%)
  between operations  1.16 us (1%)
    ppermute x10, starting transfers between devices, padded_2(): lax.ppermute(head, axis, [((i + 1) % count, i) for i in range(count)])  31.9 us
    all_gather x1, blocking collectives, on_device(): pieces = lax.all_gather(partial_value[None], 'view', axis=0, tiled=True)  25.4 us
    ppermute x10, waiting for transfers between devices, padded_2(): lax.ppermute(tail, axis, [(i, (i + 1) % count) for i in range(count)])  12.6 us
    ppermute x10, starting transfers between devices, padded_2(): lax.ppermute(tail, axis, [(i, (i + 1) % count) for i in range(count)])  8.96 us
    ppermute x10, waiting for transfers between devices, padded_2(): lax.ppermute(head, axis, [((i + 1) % count, i) for i in range(count)])  4.99 us
    mul x4, other arithmetic, advance(): open_cells[1:-1, 1:-1]  4.2 us
    concatenate x5, other arithmetic, padded_2(): jnp.concatenate([lax.ppermute(tail, axis, [(i, (i + 1) % count) for i in...  3.6 us
    unnamed x31, local copies, waits for them, and re-layouts  3.31 us
  transfers between devices with their start and end apart: 20, of which 9 were waited for; matrix products, arithmetic and copies ran while one was open for 3% of the time, Pallas kernels for 0%

commit v1 on v0

--- a/solution.py
+++ b/solution.py
@@ -108,7 +108,10 @@
     height = partial_value.shape[2]
     block_width = height // view_count
     position = lax.axis_index("view")
-    pieces = lax.all_gather(partial_value[None], "view", axis=0, tiled=True)
+    pieces = jnp.concatenate(
+        lax.all_to_all(jnp.stack([partial_value[None]] * lax.axis_size("view")), "view", 0, 0),
+        axis=0,
+    )
     mine = lax.dynamic_slice_in_dim(pieces, position * block_width, block_width, 3)
     picture = finish_pixels(fold_in_order(mine))
     return (current, picture)

time: 111 us -> 103 us (0.928)
  the two profiles are of different devices: /device:TPU:32 before, /device:TPU:31 now
where the time goes in v1:
time: 103 us; the launch traced here: 102 us
  waiting for transfers between devices  44.1 us (43%)
  starting transfers between devices  32.6 us (32%)
  other arithmetic  18.1 us (18%)
  local copies, waits for them, and re-layouts  6.04 us (6%)
  between operations  1.05 us (1%)
    ppermute x10, waiting for transfers between devices, padded_2(): lax.ppermute(head, axis, [((i + 1) % count, i) for i in range(count)])  24.1 us
    ppermute x10, starting transfers between devices, padded_2(): lax.ppermute(head, axis, [((i + 1) % count, i) for i in range(count)])  16.3 us
    all_to_all x1, waiting for transfers between devices, on_device(): lax.all_to_all(jnp.stack([partial_value[None]] * lax.axis_size('view')),...  13 us
    ppermute x10, starting transfers between devices, padded_2(): lax.ppermute(tail, axis, [(i, (i + 1) % count) for i in range(count)])  11.5 us
    ppermute x10, waiting for transfers between devices, padded_2(): lax.ppermute(tail, axis, [(i, (i + 1) % count) for i in range(count)])  6.91 us
    all_to_all x1, starting transfers between devices, on_device(): lax.all_to_all(jnp.stack([partial_value[None]] * lax.axis_size('view')),...  4.84 us
    mul x4, other arithmetic, advance(): open_cells[1:-1, 1:-1]  4.54 us
    concatenate x5, other arithmetic, padded_2(): jnp.concatenate([lax.ppermute(tail, axis, [(i, (i + 1) % count) for i in...  3.58 us
  transfers between devices with their start and end apart: 21, of which 14 were waited for; matrix products, arithmetic and copies ran while one was open for 3% of the time, Pallas kernels for 0%

profile of v1, /device:TPU:31, one launch (start us, length us, event | category | flops | bytes accessed | tf_op | source)
XLA Modules:
  0.0 102.2 jit_solution(6594224050040940230)
XLA Ops:
  1.5 5.6 %collective-permute-start.5 = (f32[1,32,128]{2,1,0:T(8,128)S(1)}, f32[1,32,128]{2,1,0:T(8,128)S(1)}, u32[]{:S(2)}, u32[]{:S(2)}) collective-permute-start(f32[1,32,128]{2,1,0:T(8,128)S(1)} %get-tuple-element.84), channel_id=1, source_target_pairs={{32,0},{64,32},{96,64},{128,96},{160,128},{192,160},{224,192},{0,2... | collective-permute-start | bytes 49160 | tf_op jit(solution)/shard_map/ppermute | solution.py:18
  7.0 1.3 %convert_bitcast_fusion = f32[1,64,32,128]{3,2,1,0:T(8,128)S(1)} fusion(s32[64,32,128]{2,1,0:T(8,128)} %param.8), kind=kLoop, calls=%fused_computation.110 | loop fusion | flops 524288 | bytes 2097152 | tf_op jit(solution)/shard_map/broadcast_in_dim | solution.py:91
  8.4 1.0 pad_maximum_fusion.13
  9.5 2.7 %collective-permute-start.1 = (f32[5,1,32,128]{3,2,1,0:T(8,128)S(1)}, f32[5,1,32,128]{3,2,1,0:T(8,128)S(1)}, u32[]{:S(2)}, u32[]{:S(2)}) collective-permute-start(f32[5,1,32,128]{3,2,1,0:T(8,128)S(1)} %get-tuple-element.45), channel_id=1, source_target_pairs={{32,0},{64,32},{96,64},{128,96},{160,128},{192,160},{224,192},{0,2... | collective-permute-start | bytes 245768 | tf_op jit(solution)/shard_map/ppermute | solution.py:18
  12.4 1.3 %collective-permute-start.6 = (f32[66,1,128]{2,1,0:T(1,128)S(1)}, f32[66,1,128]{2,1,0:T(1,128)S(1)}, u32[]{:S(2)}, u32[]{:S(2)}) collective-permute-start(f32[66,1,128]{2,1,0:T(1,128)S(1)} %get-tuple-element.76), channel_id=1, source_target_pairs={{0,1},{1,2},{2,3},{3,4},{4,5},{5,6},{6,7},{7,8},{8,9},{9,10},{10,1... | collective-permute-start | bytes 101384 | tf_op jit(solution)/shard_map/ppermute | solution.py:16
  14.4 4.8 %collective-permute-start.2 = (f32[5,66,1,128]{3,2,1,0:T(1,128)S(1)}, f32[5,66,1,128]{3,2,1,0:T(1,128)S(1)}, u32[]{:S(2)}, u32[]{:S(2)}) collective-permute-start(f32[5,66,1,128]{3,2,1,0:T(1,128)S(1)} %get-tuple-element.42), channel_id=1, source_target_pairs={{0,1},{1,2},{2,3},{3,4},{4,5},{5,6},{6,7},{7,8},{8,9},{9,10},{10,1... | collective-permute-start | bytes 506888 | tf_op jit(solution)/shard_map/ppermute | solution.py:16
  19.2 1.3 %collective-permute-done.7 = f32[66,1,128]{2,1,0:T(1,128)S(1)} collective-permute-done((f32[66,1,128]{2,1,0:T(1,128)S(1)}, f32[66,1,128]{2,1,0:T(1,128)S(1)}, u32[]{:S(2)}, u32[]{:S(2)}) %collective-permute-start.7) | collective-permute-done | bytes 33824 | tf_op jit(solution)/shard_map/ppermute | solution.py:18
  21.5 5.8 %collective-permute-done.3 = f32[5,66,1,128]{3,2,1,0:T(1,128)S(1)} collective-permute-done((f32[5,66,1,128]{3,2,1,0:T(1,128)S(1)}, f32[5,66,1,128]{3,2,1,0:T(1,128)S(1)}, u32[]{:S(2)}, u32[]{:S(2)}) %collective-permute-start.3) | collective-permute-done | bytes 168992 | tf_op jit(solution)/shard_map/ppermute | solution.py:18
  27.3 2.7 %pad_maximum_fusion.1 = f32[5,66,34,128]{3,2,1,0:T(8,128)S(1)} fusion(f32[5,66,1,128]{3,2,1,0:T(1,128)S(1)} %collective-permute-done.3, f32[5,1,32,128]{3,2,1,0:T(8,128)S(1)} %collective-permute-done.1, f32[1,64,32,128]{3,2,1,0:T(8,128)S(1)} %bitcast.45, f32[1,64,32,128]{3,2,1,0:T(8,128)S(1)} %convert_bitcast_fusion, f32[3,64,32,128]{3,2,1,0:T(8,128)S(1)} %copy-done, ...), kind=kLoop, calls=%fused_computation.7 | loop fusion | flops 8616960 | bytes 11489280 | tf_op jit(solution)/shard_map/concatenate | solution.py:14
  33.0 1.2 %fusion.37 = f32[64,32,128]{2,1,0:T(8,128)S(1)} fusion(f32[66,34,128]{2,1,0:T(8,128)S(1)} %get-tuple-element.61, f32[66,34,128]{2,1,0:T(8,128)S(1)} %get-tuple-element.60, f32[66,32,128]{2,1,0:T(8,128)S(1)} %get-tuple-element.59, f32[66,32,128]{2,1,0:T(8,128)S(1)} %get-tuple-element.58, f32[64,32,128]{2,1,0:T(8,128)S(1)} %copy-done.4, ...), kind=kLoop, calls=%fused_computation.100 | loop fusion | flops 2097152 | bytes 10485760 | tf_op jit(solution)/shard_map/mul | solution.py:42
  34.5 2.7 %collective-permute-start.9 = (f32[1,32,128]{2,1,0:T(8,128)S(1)}, f32[1,32,128]{2,1,0:T(8,128)S(1)}, u32[]{:S(2)}, u32[]{:S(2)}) collective-permute-start(f32[1,32,128]{2,1,0:T(8,128)S(1)} %get-tuple-element.83), channel_id=1, source_target_pairs={{32,0},{64,32},{96,64},{128,96},{160,128},{192,160},{224,192},{0,2... | collective-permute-start | bytes 49160 | tf_op jit(solution)/shard_map/ppermute | solution.py:18
  37.2 1.1 %collective-permute-done.8 = f32[1,32,128]{2,1,0:T(8,128)S(1)} collective-permute-done((f32[1,32,128]{2,1,0:T(8,128)S(1)}, f32[1,32,128]{2,1,0:T(8,128)S(1)}, u32[]{:S(2)}, u32[]{:S(2)}) %collective-permute-start.8) | collective-permute-done | bytes 16416 | tf_op jit(solution)/shard_map/ppermute | solution.py:16
  38.3 1.2 %collective-permute-start.10 = (f32[66,1,128]{2,1,0:T(1,128)S(1)}, f32[66,1,128]{2,1,0:T(1,128)S(1)}, u32[]{:S(2)}, u32[]{:S(2)}) collective-permute-start(f32[66,1,128]{2,1,0:T(1,128)S(1)} %get-tuple-element.74), channel_id=1, source_target_pairs={{0,1},{1,2},{2,3},{3,4},{4,5},{5,6},{6,7},{7,8},{8,9},{9,10},{10,1... | collective-permute-start | bytes 101384 | tf_op jit(solution)/shard_map/ppermute | solution.py:16
  39.6 1.0 %collective-permute-done.10 = f32[66,1,128]{2,1,0:T(1,128)S(1)} collective-permute-done((f32[66,1,128]{2,1,0:T(1,128)S(1)}, f32[66,1,128]{2,1,0:T(1,128)S(1)}, u32[]{:S(2)}, u32[]{:S(2)}) %collective-permute-start.10) | collective-permute-done | bytes 33824 | tf_op jit(solution)/shard_map/ppermute | solution.py:16
  40.6 5.6 %collective-permute-done.11 = f32[66,1,128]{2,1,0:T(1,128)S(1)} collective-permute-done((f32[66,1,128]{2,1,0:T(1,128)S(1)}, f32[66,1,128]{2,1,0:T(1,128)S(1)}, u32[]{:S(2)}, u32[]{:S(2)}) %collective-permute-start.11) | collective-permute-done | bytes 33824 | tf_op jit(solution)/shard_map/ppermute | solution.py:18
  48.4 1.1 %fusion.32 = f32[64,32,128]{2,1,0:T(8,128)S(1)} fusion(f32[66,34,128]{2,1,0:T(8,128)S(1)} %get-tuple-element.57, f32[66,34,128]{2,1,0:T(8,128)S(1)} %get-tuple-element.56, f32[66,32,128]{2,1,0:T(8,128)S(1)} %get-tuple-element.55, f32[66,32,128]{2,1,0:T(8,128)S(1)} %get-tuple-element.54, f32[64,32,128]{2,1,0:T(8,128)S(1)} %fusion.37, ...), kind=kLoop, calls=%fused_computation.92 | loop fusion | flops 2097152 | bytes 10485760 | tf_op jit(solution)/shard_map/mul | solution.py:42
  49.7 3.0 %collective-permute-start.13 = (f32[1,32,128]{2,1,0:T(8,128)S(1)}, f32[1,32,128]{2,1,0:T(8,128)S(1)}, u32[]{:S(2)}, u32[]{:S(2)}) collective-permute-start(f32[1,32,128]{2,1,0:T(8,128)S(1)} %get-tuple-element.81), channel_id=1, source_target_pairs={{32,0},{64,32},{96,64},{128,96},{160,128},{192,160},{224,192},{0,2... | collective-permute-start | bytes 49160 | tf_op jit(solution)/shard_map/ppermute | solution.py:18
  52.7 1.0 %collective-permute-done.12 = f32[1,32,128]{2,1,0:T(8,128)S(1)} collective-permute-done((f32[1,32,128]{2,1,0:T(8,128)S(1)}, f32[1,32,128]{2,1,0:T(8,128)S(1)}, u32[]{:S(2)}, u32[]{:S(2)}) %collective-permute-start.12) | collective-permute-done | bytes 16416 | tf_op jit(solution)/shard_map/ppermute | solution.py:16
  53.8 1.0 collective-permute-start.14
  54.7 1.0 %collective-permute-done.14 = f32[66,1,128]{2,1,0:T(1,128)S(1)} collective-permute-done((f32[66,1,128]{2,1,0:T(1,128)S(1)}, f32[66,1,128]{2,1,0:T(1,128)S(1)}, u32[]{:S(2)}, u32[]{:S(2)}) %collective-permute-start.14) | collective-permute-done | bytes 33824 | tf_op jit(solution)/shard_map/ppermute | solution.py:16
  55.8 5.6 %collective-permute-done.15 = f32[66,1,128]{2,1,0:T(1,128)S(1)} collective-permute-done((f32[66,1,128]{2,1,0:T(1,128)S(1)}, f32[66,1,128]{2,1,0:T(1,128)S(1)}, u32[]{:S(2)}, u32[]{:S(2)}) %collective-permute-start.15) | collective-permute-done | bytes 33824 | tf_op jit(solution)/shard_map/ppermute | solution.py:18
  63.6 1.1 %fusion.27 = f32[64,32,128]{2,1,0:T(8,128)S(1)} fusion(f32[66,34,128]{2,1,0:T(8,128)S(1)} %get-tuple-element.53, f32[66,34,128]{2,1,0:T(8,128)S(1)} %get-tuple-element.52, f32[66,32,128]{2,1,0:T(8,128)S(1)} %get-tuple-element.51, f32[66,32,128]{2,1,0:T(8,128)S(1)} %get-tuple-element.50, f32[64,32,128]{2,1,0:T(8,128)S(1)} %fusion.32, ...), kind=kLoop, calls=%fused_computation.84 | loop fusion | flops 2097152 | bytes 10485760 | tf_op jit(solution)/shard_map/mul | solution.py:42
  64.7 1.5 %collective-permute-start.16 = (f32[1,32,128]{2,1,0:T(8,128)S(1)}, f32[1,32,128]{2,1,0:T(8,128)S(1)}, u32[]{:S(2)}, u32[]{:S(2)}) collective-permute-start(f32[1,32,128]{2,1,0:T(8,128)S(1)} %get-tuple-element.78), channel_id=1, source_target_pairs={{0,32},{32,64},{64,96},{96,128},{128,160},{160,192},{192,224},{224... | collective-permute-start | bytes 49160 | tf_op jit(solution)/shard_map/ppermute | solution.py:16
  66.3 1.9 %collective-permute-start.17 = (f32[1,32,128]{2,1,0:T(8,128)S(1)}, f32[1,32,128]{2,1,0:T(8,128)S(1)}, u32[]{:S(2)}, u32[]{:S(2)}) collective-permute-start(f32[1,32,128]{2,1,0:T(8,128)S(1)} %get-tuple-element.79), channel_id=1, source_target_pairs={{32,0},{64,32},{96,64},{128,96},{160,128},{192,160},{224,192},{0,2... | collective-permute-start | bytes 49160 | tf_op jit(solution)/shard_map/ppermute | solution.py:18
  69.2 1.2 %collective-permute-start.18 = (f32[66,1,128]{2,1,0:T(1,128)S(1)}, f32[66,1,128]{2,1,0:T(1,128)S(1)}, u32[]{:S(2)}, u32[]{:S(2)}) collective-permute-start(f32[66,1,128]{2,1,0:T(1,128)S(1)} %get-tuple-element.70), channel_id=1, source_target_pairs={{0,1},{1,2},{2,3},{3,4},{4,5},{5,6},{6,7},{7,8},{8,9},{9,10},{10,1... | collective-permute-start | bytes 101384 | tf_op jit(solution)/shard_map/ppermute | solution.py:16
  70.4 1.0 %collective-permute-done.18 = f32[66,1,128]{2,1,0:T(1,128)S(1)} collective-permute-done((f32[66,1,128]{2,1,0:T(1,128)S(1)}, f32[66,1,128]{2,1,0:T(1,128)S(1)}, u32[]{:S(2)}, u32[]{:S(2)}) %collective-permute-start.18) | collective-permute-done | bytes 33824 | tf_op jit(solution)/shard_map/ppermute | solution.py:16
  71.4 5.6 %collective-permute-done.19 = f32[66,1,128]{2,1,0:T(1,128)S(1)} collective-permute-done((f32[66,1,128]{2,1,0:T(1,128)S(1)}, f32[66,1,128]{2,1,0:T(1,128)S(1)}, u32[]{:S(2)}, u32[]{:S(2)}) %collective-permute-start.19) | collective-permute-done | bytes 33824 | tf_op jit(solution)/shard_map/ppermute | solution.py:18
  79.3 1.1 %fusion.22 = f32[64,32,128]{2,1,0:T(8,128)S(1)} fusion(f32[66,34,128]{2,1,0:T(8,128)S(1)} %get-tuple-element.49, f32[66,34,128]{2,1,0:T(8,128)S(1)} %get-tuple-element.48, f32[66,32,128]{2,1,0:T(8,128)S(1)} %get-tuple-element.47, f32[66,32,128]{2,1,0:T(8,128)S(1)} %get-tuple-element.46, f32[64,32,128]{2,1,0:T(8,128)S(1)} %fusion.27, ...), kind=kLoop, calls=%fused_computation.76 | loop fusion | flops 2097152 | bytes 10485760 | tf_op jit(solution)/shard_map/mul | solution.py:42
  80.5 1.4 %multiply_reduce_fusion.1 = (f32[32,128]{1,0:T(8,128)S(1)}, f32[32,128]{1,0:T(8,128)S(1)}, f32[32,128]{1,0:T(8,128)S(1)}, f32[32,128]{1,0:T(8,128)S(1)}) fusion(s32[64,32,128]{2,1,0:T(8,128)S(1)} %copy-done.2, f32[64,32,128]{2,1,0:T(8,128)S(1)} %fusion.22), kind=kOutput, calls=%fused_computation.106 | output fusion | flops 27246592 | bytes 2162688 | tf_op jit(solution)/shard_map/jit(cumsum)/reduce_window_sum | solution.py:97
  81.9 0.8 stack.20
  82.7 4.8 %all-to-all-start = ((f32[8,1,4,32,128]{4,3,2,1,0:T(8,128)}), f32[8,1,4,32,128]{4,3,2,1,0:T(8,128)S(1)}, u32[]{:S(2)}, u32[]{:S(2)}) async-start(f32[8,1,4,32,128]{4,3,2,1,0:T(8,128)} %stack.20), calls=%async_computation | async-start | bytes 1048576 | tf_op jit(solution)/shard_map/all_to_all | solution.py:112
  87.6 13.0 %all-to-all-done = f32[8,1,4,32,128]{4,3,2,1,0:T(8,128)S(1)} async-done(((f32[8,1,4,32,128]{4,3,2,1,0:T(8,128)}), f32[8,1,4,32,128]{4,3,2,1,0:T(8,128)S(1)}, u32[]{:S(2)}, u32[]{:S(2)}) %all-to-all-start) | async-done | bytes 524320 | tf_op jit(solution)/shard_map/all_to_all | solution.py:112
  (104 shorter events, 15.5 us)
Async XLA Ops:
  0.6 7.8 %copy-start.3 = (f32[64,32,128]{2,1,0:T(8,128)S(1)}, f32[64,32,128]{2,1,0:T(8,128)}, u32[]{:S(2)}) copy-start(f32[64,32,128]{2,1,0:T(8,128)} %param.9) | copy-start | bytes 3145732
  1.5 10.9 %collective-permute-start.5 = (f32[1,32,128]{2,1,0:T(8,128)S(1)}, f32[1,32,128]{2,1,0:T(8,128)S(1)}, u32[]{:S(2)}, u32[]{:S(2)}) collective-permute-start(f32[1,32,128]{2,1,0:T(8,128)S(1)} %get-tuple-element.84), channel_id=1, source_target_pairs={{32,0},{64,32},{96,64},{128,96},{160,128},{192,160},{224,192},{0,2... | collective-permute-start | bytes 49160 | tf_op jit(solution)/shard_map/ppermute | solution.py:18
  7.0 5.2 %collective-permute-start.4 = (f32[1,32,128]{2,1,0:T(8,128)S(1)}, f32[1,32,128]{2,1,0:T(8,128)S(1)}, u32[]{:S(2)}, u32[]{:S(2)}) collective-permute-start(f32[1,32,128]{2,1,0:T(8,128)S(1)} %get-tuple-element.85), channel_id=1, source_target_pairs={{0,32},{32,64},{64,96},{96,128},{128,160},{160,192},{192,224},{224... | collective-permute-start | bytes 49160 | tf_op jit(solution)/shard_map/ppermute | solution.py:16
  8.4 3.9 %copy-start.4 = (f32[64,32,128]{2,1,0:T(8,128)S(1)}, f32[64,32,128]{2,1,0:T(8,128)}, u32[]{:S(2)}) copy-start(f32[64,32,128]{2,1,0:T(8,128)} %param.6) | copy-start | bytes 3145732
  8.4 5.7 %copy-start = (f32[3,64,32,128]{3,2,1,0:T(8,128)S(1)}, f32[3,64,32,128]{3,2,1,0:T(8,128)}, u32[]{:S(2)}) copy-start(f32[3,64,32,128]{3,2,1,0:T(8,128)} %param.7) | copy-start | bytes 9437188
  9.4 4.7 %collective-permute-start = (f32[5,1,32,128]{3,2,1,0:T(8,128)S(1)}, f32[5,1,32,128]{3,2,1,0:T(8,128)S(1)}, u32[]{:S(2)}, u32[]{:S(2)}) collective-permute-start(f32[5,1,32,128]{3,2,1,0:T(8,128)S(1)} %get-tuple-element.44), channel_id=1, source_target_pairs={{0,32},{32,64},{64,96},{96,128},{128,160},{160,192},{192,224},{224... | collective-permute-start | bytes 245768 | tf_op jit(solution)/shard_map/ppermute | solution.py:16
  9.5 4.6 %collective-permute-start.1 = (f32[5,1,32,128]{3,2,1,0:T(8,128)S(1)}, f32[5,1,32,128]{3,2,1,0:T(8,128)S(1)}, u32[]{:S(2)}, u32[]{:S(2)}) collective-permute-start(f32[5,1,32,128]{3,2,1,0:T(8,128)S(1)} %get-tuple-element.45), channel_id=1, source_target_pairs={{32,0},{64,32},{96,64},{128,96},{160,128},{192,160},{224,192},{0,2... | collective-permute-start | bytes 245768 | tf_op jit(solution)/shard_map/ppermute | solution.py:18
  12.4 6.7 %collective-permute-start.6 = (f32[66,1,128]{2,1,0:T(1,128)S(1)}, f32[66,1,128]{2,1,0:T(1,128)S(1)}, u32[]{:S(2)}, u32[]{:S(2)}) collective-permute-start(f32[66,1,128]{2,1,0:T(1,128)S(1)} %get-tuple-element.76), channel_id=1, source_target_pairs={{0,1},{1,2},{2,3},{3,4},{4,5},{5,6},{6,7},{7,8},{8,9},{9,10},{10,1... | collective-permute-start | bytes 101384 | tf_op jit(solution)/shard_map/ppermute | solution.py:16
  13.8 6.7 %collective-permute-start.7 = (f32[66,1,128]{2,1,0:T(1,128)S(1)}, f32[66,1,128]{2,1,0:T(1,128)S(1)}, u32[]{:S(2)}, u32[]{:S(2)}) collective-permute-start(f32[66,1,128]{2,1,0:T(1,128)S(1)} %get-tuple-element.77), channel_id=1, source_target_pairs={{1,0},{2,1},{3,2},{4,3},{5,4},{6,5},{7,6},{8,7},{9,8},{10,9},{11,1... | collective-permute-start | bytes 101384 | tf_op jit(solution)/shard_map/ppermute | solution.py:18
  14.4 7.1 %collective-permute-start.2 = (f32[5,66,1,128]{3,2,1,0:T(1,128)S(1)}, f32[5,66,1,128]{3,2,1,0:T(1,128)S(1)}, u32[]{:S(2)}, u32[]{:S(2)}) collective-permute-start(f32[5,66,1,128]{3,2,1,0:T(1,128)S(1)} %get-tuple-element.42), channel_id=1, source_target_pairs={{0,1},{1,2},{2,3},{3,4},{4,5},{5,6},{6,7},{7,8},{8,9},{9,10},{10,1... | collective-permute-start | bytes 506888 | tf_op jit(solution)/shard_map/ppermute | solution.py:16
  19.2 8.1 %collective-permute-start.3 = (f32[5,66,1,128]{3,2,1,0:T(1,128)S(1)}, f32[5,66,1,128]{3,2,1,0:T(1,128)S(1)}, u32[]{:S(2)}, u32[]{:S(2)}) collective-permute-start(f32[5,66,1,128]{3,2,1,0:T(1,128)S(1)} %get-tuple-element.43), channel_id=1, source_target_pairs={{1,0},{2,1},{3,2},{4,3},{5,4},{6,5},{7,6},{8,7},{9,8},{10,9},{11,1... | collective-permute-start | bytes 506888 | tf_op jit(solution)/shard_map/ppermute | solution.py:18
  34.2 4.1 %collective-permute-start.8 = (f32[1,32,128]{2,1,0:T(8,128)S(1)}, f32[1,32,128]{2,1,0:T(8,128)S(1)}, u32[]{:S(2)}, u32[]{:S(2)}) collective-permute-start(f32[1,32,128]{2,1,0:T(8,128)S(1)} %get-tuple-element.82), channel_id=1, source_target_pairs={{0,32},{32,64},{64,96},{96,128},{128,160},{160,192},{192,224},{224... | collective-permute-start | bytes 49160 | tf_op jit(solution)/shard_map/ppermute | solution.py:16
  34.5 3.8 %collective-permute-start.9 = (f32[1,32,128]{2,1,0:T(8,128)S(1)}, f32[1,32,128]{2,1,0:T(8,128)S(1)}, u32[]{:S(2)}, u32[]{:S(2)}) collective-permute-start(f32[1,32,128]{2,1,0:T(8,128)S(1)} %get-tuple-element.83), channel_id=1, source_target_pairs={{32,0},{64,32},{96,64},{128,96},{160,128},{192,160},{224,192},{0,2... | collective-permute-start | bytes 49160 | tf_op jit(solution)/shard_map/ppermute | solution.py:18
  38.3 2.3 %collective-permute-start.10 = (f32[66,1,128]{2,1,0:T(1,128)S(1)}, f32[66,1,128]{2,1,0:T(1,128)S(1)}, u32[]{:S(2)}, u32[]{:S(2)}) collective-permute-start(f32[66,1,128]{2,1,0:T(1,128)S(1)} %get-tuple-element.74), channel_id=1, source_target_pairs={{0,1},{1,2},{2,3},{3,4},{4,5},{5,6},{6,7},{7,8},{8,9},{9,10},{10,1... | collective-permute-start | bytes 101384 | tf_op jit(solution)/shard_map/ppermute | solution.py:16
  39.6 6.7 %collective-permute-start.11 = (f32[66,1,128]{2,1,0:T(1,128)S(1)}, f32[66,1,128]{2,1,0:T(1,128)S(1)}, u32[]{:S(2)}, u32[]{:S(2)}) collective-permute-start(f32[66,1,128]{2,1,0:T(1,128)S(1)} %get-tuple-element.75), channel_id=1, source_target_pairs={{1,0},{2,1},{3,2},{4,3},{5,4},{6,5},{7,6},{8,7},{9,8},{10,9},{11,1... | collective-permute-start | bytes 101384 | tf_op jit(solution)/shard_map/ppermute | solution.py:18
  49.6 4.2 %collective-permute-start.12 = (f32[1,32,128]{2,1,0:T(8,128)S(1)}, f32[1,32,128]{2,1,0:T(8,128)S(1)}, u32[]{:S(2)}, u32[]{:S(2)}) collective-permute-start(f32[1,32,128]{2,1,0:T(8,128)S(1)} %get-tuple-element.80), channel_id=1, source_target_pairs={{0,32},{32,64},{64,96},{96,128},{128,160},{160,192},{192,224},{224... | collective-permute-start | bytes 49160 | tf_op jit(solution)/shard_map/ppermute | solution.py:16
  49.7 4.1 %collective-permute-start.13 = (f32[1,32,128]{2,1,0:T(8,128)S(1)}, f32[1,32,128]{2,1,0:T(8,128)S(1)}, u32[]{:S(2)}, u32[]{:S(2)}) collective-permute-start(f32[1,32,128]{2,1,0:T(8,128)S(1)} %get-tuple-element.81), channel_id=1, source_target_pairs={{32,0},{64,32},{96,64},{128,96},{160,128},{192,160},{224,192},{0,2... | collective-permute-start | bytes 49160 | tf_op jit(solution)/shard_map/ppermute | solution.py:18
  53.8 2.0 %collective-permute-start.14 = (f32[66,1,128]{2,1,0:T(1,128)S(1)}, f32[66,1,128]{2,1,0:T(1,128)S(1)}, u32[]{:S(2)}, u32[]{:S(2)}) collective-permute-start(f32[66,1,128]{2,1,0:T(1,128)S(1)} %get-tuple-element.72), channel_id=1, source_target_pairs={{0,1},{1,2},{2,3},{3,4},{4,5},{5,6},{6,7},{7,8},{8,9},{9,10},{10,1... | collective-permute-start | bytes 101384 | tf_op jit(solution)/shard_map/ppermute | solution.py:16
  54.7 6.7 %collective-permute-start.15 = (f32[66,1,128]{2,1,0:T(1,128)S(1)}, f32[66,1,128]{2,1,0:T(1,128)S(1)}, u32[]{:S(2)}, u32[]{:S(2)}) collective-permute-start(f32[66,1,128]{2,1,0:T(1,128)S(1)} %get-tuple-element.73), channel_id=1, source_target_pairs={{1,0},{2,1},{3,2},{4,3},{5,4},{6,5},{7,6},{8,7},{9,8},{10,9},{11,1... | collective-permute-start | bytes 101384 | tf_op jit(solution)/shard_map/ppermute | solution.py:18
  64.7 4.2 %collective-permute-start.16 = (f32[1,32,128]{2,1,0:T(8,128)S(1)}, f32[1,32,128]{2,1,0:T(8,128)S(1)}, u32[]{:S(2)}, u32[]{:S(2)}) collective-permute-start(f32[1,32,128]{2,1,0:T(8,128)S(1)} %get-tuple-element.78), channel_id=1, source_target_pairs={{0,32},{32,64},{64,96},{96,128},{128,160},{160,192},{192,224},{224... | collective-permute-start | bytes 49160 | tf_op jit(solution)/shard_map/ppermute | solution.py:16
  66.3 2.9 %collective-permute-start.17 = (f32[1,32,128]{2,1,0:T(8,128)S(1)}, f32[1,32,128]{2,1,0:T(8,128)S(1)}, u32[]{:S(2)}, u32[]{:S(2)}) collective-permute-start(f32[1,32,128]{2,1,0:T(8,128)S(1)} %get-tuple-element.79), channel_id=1, source_target_pairs={{32,0},{64,32},{96,64},{128,96},{160,128},{192,160},{224,192},{0,2... | collective-permute-start | bytes 49160 | tf_op jit(solution)/shard_map/ppermute | solution.py:18
  69.2 2.3 %collective-permute-start.18 = (f32[66,1,128]{2,1,0:T(1,128)S(1)}, f32[66,1,128]{2,1,0:T(1,128)S(1)}, u32[]{:S(2)}, u32[]{:S(2)}) collective-permute-start(f32[66,1,128]{2,1,0:T(1,128)S(1)} %get-tuple-element.70), channel_id=1, source_target_pairs={{0,1},{1,2},{2,3},{3,4},{4,5},{5,6},{6,7},{7,8},{8,9},{9,10},{10,1... | collective-permute-start | bytes 101384 | tf_op jit(solution)/shard_map/ppermute | solution.py:16
  70.4 6.7 %collective-permute-start.19 = (f32[66,1,128]{2,1,0:T(1,128)S(1)}, f32[66,1,128]{2,1,0:T(1,128)S(1)}, u32[]{:S(2)}, u32[]{:S(2)}) collective-permute-start(f32[66,1,128]{2,1,0:T(1,128)S(1)} %get-tuple-element.71), channel_id=1, source_target_pairs={{1,0},{2,1},{3,2},{4,3},{5,4},{6,5},{7,6},{8,7},{9,8},{10,9},{11,1... | collective-permute-start | bytes 101384 | tf_op jit(solution)/shard_map/ppermute | solution.py:18
  79.3 1.2 %copy-start.2 = (s32[64,32,128]{2,1,0:T(8,128)S(1)}, s32[64,32,128]{2,1,0:T(8,128)}, u32[]{:S(2)}) copy-start(s32[64,32,128]{2,1,0:T(8,128)} %param.8) | copy-start | bytes 3145732
  80.5 1.4 %copy-start.1 = (f32[64,32,128]{2,1,0:T(8,128)}, f32[64,32,128]{2,1,0:T(8,128)S(1)}, u32[]{:S(2)}) copy-start(f32[64,32,128]{2,1,0:T(8,128)S(1)} %fusion.22) | copy-start | bytes 3145732
  82.7 18.3 %copy-start.5 = (f32[4,32,16]{1,2,0:T(8,128)S(1)}, f32[4,32,16]{1,2,0:T(8,128)}, u32[]{:S(2)}) copy-start(f32[4,32,16]{1,2,0:T(8,128)} %constant.10.clone.1) | copy-start | bytes 24580
  82.7 17.9 %all-to-all-start = ((f32[8,1,4,32,128]{4,3,2,1,0:T(8,128)}), f32[8,1,4,32,128]{4,3,2,1,0:T(8,128)S(1)}, u32[]{:S(2)}, u32[]{:S(2)}) async-start(f32[8,1,4,32,128]{4,3,2,1,0:T(8,128)} %stack.20), calls=%async_computation | async-start | bytes 1048576 | tf_op jit(solution)/shard_map/all_to_all | solution.py:112
